TPU v7x, 256 devices: a whole 4x4x8 slice. The times are simulated.
256 devices in a mesh: slide: 16 (over x, y_hi, core), rep: 16 (over z, y_lo).
Axes of the slice: x: 4, y: 4 (y_hi: 2, y_lo: 2; y = y_hi * 2 + y_lo), z: 8, core: 2. Of those that a mesh axis runs over, the one named last changes fastest.
Arguments:
- tile_images: bfloat16 [1024, 32, 32, 384], P(('slide', 'rep')), may hold values from -6 to 6
- cotangent: bfloat16 [1024, 32, 32, 384], P(('slide', 'rep')), may hold values from -0.1875 to 0.1875
- depth_kernel: bfloat16 [7, 7, 384], replicated, may hold values from -0.875 to 0.875
- depth_bias: float32 [384], replicated, may hold values from -3 to 3
- norm_gain: float32 [384], replicated, may hold values from 0.5 to 2
- norm_bias: float32 [384], replicated, may hold values from -3 to 3
- expand_weight: bfloat16 [1536, 384], replicated, may hold values from -0.3125 to 0.3125
- expand_bias: float32 [1536], replicated, may hold values from -3 to 3
- project_weight: bfloat16 [1536, 384], replicated, may hold values from -0.15625 to 0.15625
- layer_scale: float32 [384], replicated, may hold values from 0.1 to 1
- tile_counts: int32 [16, 16], P('slide', 'rep'), may hold values from 1 to 4, as said below
- send_list: int32 [16, 16, 16], P('slide', 'rep'), may hold values from -1 to 31, as said below
Outputs:
- grad_expand: float32 [1536, 384], P(('slide', 'rep'))
- grad_project: float32 [1536, 384], P(('slide', 'rep'))
Inputs may be any that keep to these rules, and one draw needn't show every extreme that they name: Every device holds its tiles in its first tile_counts slots; some device holds 4 tiles and some device one. `send_list`: the blocks that a device names are distinct and lie in its first tile_counts tiles; each device names at least one block and at most 16, at most one for each destination, and some device names 16; each device (d, r) is named as destination by at most 5 devices, and some device by exactly 5.
All inputs are finite; a program needn't handle non-finite values.
Results may differ from a plain program's by a relative error of at most 0.0055.
Values may be sent and summed in bfloat16 or wider, within the bound.
No kernel may reach another device: no remote copies, remote signals or barrier semaphores. Data moves between devices by JAX's collectives and lax.ppermute only.
A program may use at most 128 MiB of HBM per device.

v0:
```python
import jax
import jax.numpy as jnp
from jax import lax
from jax.sharding import PartitionSpec as P

RECV_MOST = 5
BANDS = 8
BAND_TOK = 128


root_half = 0.7071067811865476
inv_root_tau = 0.3989422804014327


def gelu_value(pre_act):
    return 0.5 * pre_act * (1.0 + lax.erf(pre_act * root_half))


def gelu_slope(pre_act):
    return (
        0.5 * (1.0 + lax.erf(pre_act * root_half))
        + pre_act * jnp.exp(-0.5 * pre_act * pre_act) * inv_root_tau
    )


def prepare(
    tile_images, cotangent, held_count, depth_kernel, depth_bias, norm_gain, norm_bias, layer_scale
):
    channels = tile_images.shape[-1]
    kernel_size = depth_kernel.shape[0]
    kernel = depth_kernel.reshape(kernel_size, kernel_size, 1, channels)
    margin = kernel_size // 2
    mixed_conv = lax.conv_general_dilated(
        tile_images,
        kernel,
        (1, 1),
        ((margin, margin), (margin, margin)),
        dimension_numbers=("NHWC", "HWIO", "NHWC"),
        feature_group_count=channels,
        preferred_element_type=jnp.float32,
    )
    mixed_conv = mixed_conv + depth_bias
    centre = jnp.mean(mixed_conv, axis=-1, keepdims=True)
    spread = jnp.mean(jnp.square(mixed_conv - centre), axis=-1, keepdims=True)
    normed = ((mixed_conv - centre) * lax.rsqrt(spread + 1e-06) * norm_gain + norm_bias).astype(
        jnp.bfloat16
    )
    scaled = (
        cotangent.astype(jnp.float32) * (layer_scale / held_count.astype(jnp.float32))
    ).astype(jnp.bfloat16)
    block_total = tile_images.shape[0] * BANDS
    return (
        normed.reshape(block_total, BAND_TOK, channels),
        scaled.reshape(block_total, BAND_TOK, channels),
    )


def reduce_rows(term_fn, hidden_total):
    keep_rows = hidden_total // (lax.axis_size("slide") * lax.axis_size("rep"))
    summed = lax.psum_scatter(
        term_fn(jnp.int32(0), keep_rows * lax.axis_size(("slide", "rep"))),
        ("slide", "rep"),
        scatter_dimension=0,
        tiled=True,
    )
    return summed


def per_device(
    tile_images,
    cotangent,
    depth_kernel,
    depth_bias,
    norm_gain,
    norm_bias,
    expand_weight,
    expand_bias,
    project_weight,
    layer_scale,
    tile_counts,
    send_list,
):
    slot_ids = send_list.reshape(-1)
    held_count = tile_counts.reshape(())
    normed, scaled = prepare(
        tile_images,
        cotangent,
        held_count,
        depth_kernel,
        depth_bias,
        norm_gain,
        norm_bias,
        layer_scale,
    )
    block_total = normed.shape[0]
    slot_total = slot_ids.shape[0]
    chosen = jnp.clip(slot_ids, 0, block_total - 1)
    live_slot = slot_ids >= 0
    send_in = jnp.take(normed, chosen, axis=0)
    send_err = jnp.where(
        live_slot[:, None, None],
        jnp.take(scaled, chosen, axis=0),
        jnp.zeros((slot_total,) + scaled.shape[1:], scaled.dtype),
    )
    flags = live_slot.astype(jnp.bfloat16)
    got_in, got_err, got_flags = (
        lax.all_to_all(send_in, "slide", split_axis=0, concat_axis=0, tiled=True),
        lax.all_to_all(send_err, "slide", split_axis=0, concat_axis=0, tiled=True),
        lax.all_to_all(flags, "slide", split_axis=0, concat_axis=0, tiled=True),
    )
    slot_index = jnp.arange(slot_total, dtype=jnp.int32)
    order_keys = jnp.where(got_flags > 0, 0, 1).astype(jnp.int32) * slot_total + slot_index
    keep = jnp.argsort(order_keys, stable=True)[:RECV_MOST]
    rows_in = jnp.take(got_in, keep, axis=0)
    rows_err = jnp.take(got_err, keep, axis=0)
    channels = rows_in.shape[-1]
    flat_in = rows_in.reshape(-1, channels)
    flat_err = rows_err.reshape(-1, channels)
    inner_dims = (((1,), (1,)), ((), ()))
    outer_dims = (((0,), (0,)), ((), ()))
    pre_act = (
        lax.dot_general(flat_in, expand_weight, inner_dims, preferred_element_type=jnp.float32)
        + expand_bias
    )
    activated = gelu_value(pre_act).astype(jnp.bfloat16)
    hidden_total = expand_weight.shape[0]

    def project_term(first_row, row_count):
        return lax.dot_general(activated, flat_err, outer_dims, preferred_element_type=jnp.float32)

    grad_project = reduce_rows(project_term, hidden_total)
    back_grad = lax.dot_general(
        flat_err, project_weight, inner_dims, preferred_element_type=jnp.float32
    )
    slope_term = (back_grad * gelu_slope(pre_act)).astype(jnp.bfloat16)

    def expand_term(first_row, row_count):
        return lax.dot_general(slope_term, flat_in, outer_dims, preferred_element_type=jnp.float32)

    grad_expand = reduce_rows(expand_term, hidden_total)
    return (grad_expand, grad_project)


def solution(mesh):
    in_specs = (
        P(("slide", "rep"), None, None, None),
        P(("slide", "rep"), None, None, None),
        P(),
        P(),
        P(),
        P(),
        P(),
        P(),
        P(),
        P(),
        P("slide", "rep"),
        P("slide", "rep", None),
    )
    out_specs = (P(("slide", "rep"), None), P(("slide", "rep"), None))
    return jax.shard_map(
        per_device, mesh=mesh, in_specs=in_specs, out_specs=out_specs, check_vma=False
    )
```

profile of v0, /device:TPU:2, one launch (start us, length us, event | category | flops | bytes accessed | tf_op | source)
XLA Modules:
  0.0 425.8 jit_solution(17311023625777428346)
XLA Ops:
  7.2 0.0 copy-start
  7.2 0.8 compare_bitcast_fusion
  7.9 0.7 copy.23
  8.6 7.5 %all-to-all-start.1 = ((bf16[16,1,1]{2,1,0:T(2,128)(2,1)}), bf16[16,1,1]{2,1,0:T(2,128)(2,1)S(1)}, u32[]{:S(2)}, u32[]{:S(2)}) async-start(bf16[16,1,1]{2,1,0:T(2,128)(2,1)} %copy.23), calls=%async_computation.1 | async-start | bytes 16384 | tf_op jit(solution)/shard_map/all_to_all | solution.py:109
  16.1 0.7 compare_and_fusion.1
  16.8 0.0 copy-start.3
  16.8 32.6 %add_reduce_fusion = (f32[4,32,32]{0,2,1:T(8,128)S(1)}, f32[4,32,32,384]{3,0,2,1:T(4,128)S(1)}) fusion(f32[384]{0:T(512)} %param.19, bf16[7,7,1,384]{3,1,0,2:T(8,128)(2,1)} %bitcast.25, bf16[4,32,32,384]{3,2,1,0:T(8,128)(2,1)} %param.16), kind=kOutput, calls=%fused_computation.8 | convolution fusion | flops 141209600 | bytes 9492736 | tf_op jit(solution)/shard_map/conv_general_dilated | solution.py:33
  49.3 0.1 broadcast_multiply_fusion
  49.4 0.0 copy-done.3
  49.4 0.0 copy-start.5
  49.4 0.0 copy-start.6
  49.4 3.3 multiply_reduce_fusion
  52.7 0.1 add_rsqrt_fusion
  52.8 0.0 copy-done.5
  52.8 0.0 copy-done.6
  52.8 2.9 add_convert_fusion
  55.7 0.0 copy-start.4
  55.8 2.1 copy.26
  58.6 3.8 gather_fusion.2
  62.4 0.0 copy-done.4
  62.4 4.2 multiply_convert_fusion
  66.5 3.8 gather_fusion
  70.4 3.5 select_select_fusion
  73.9 0.0 all-to-all-done.1
  73.9 28.3 %all_to_all.16 = bf16[16,128,384]{2,1,0:T(8,128)(2,1)} all-to-all(bf16[16,128,384]{2,1,0:T(8,128)(2,1)S(1)} %get-tuple-element.15), channel_id=1, replica_groups=mesh['slide'=16,'rep'=16] {'slide'}, dimensions={0} | all-to-all | bytes 3145728 | tf_op jit(solution)/shard_map/all_to_all | solution.py:107
  102.2 0.0 copy-start.2
  102.2 6.1 %all-to-all-start = ((bf16[16,128,384]{2,1,0:T(8,128)(2,1)}), bf16[16,128,384]{2,1,0:T(8,128)(2,1)S(1)}, u32[]{:S(2)}, u32[]{:S(2)}) async-start(bf16[16,128,384]{2,1,0:T(8,128)(2,1)} %get-tuple-element.14), calls=%async_computation | async-start | bytes 3145728 | tf_op jit(solution)/shard_map/all_to_all | solution.py:108
  108.3 0.2 all-reduce.5.cloned.1.call-start
  108.6 0.4 fusion.13
  109.0 1.2 sort.17
  110.2 2.1 gather_fusion.3
  112.3 18.0 %all-to-all-done = bf16[16,128,384]{2,1,0:T(8,128)(2,1)S(1)} async-done(((bf16[16,128,384]{2,1,0:T(8,128)(2,1)}), bf16[16,128,384]{2,1,0:T(8,128)(2,1)S(1)}, u32[]{:S(2)}, u32[]{:S(2)}) %all-to-all-start) | async-done | bytes 1572896 | tf_op jit(solution)/shard_map/all_to_all | solution.py:108
  130.3 1.4 gather_fusion.1
  131.7 1.2 broadcast_select_fusion.2
  132.9 0.0 copy-done
  132.9 0.0 copy-done.2
  132.9 1.2 convolution_add_fusion
  134.1 0.0 copy-start.1
  134.1 1.9 copy-done.1
  136.0 0.0 copy-start.7
  136.0 2.6 fusion.8
  138.7 0.0 copy-done.7
  138.7 6.3 %fusion.10 = f32[1536,384]{1,0:T(8,128)} fusion(bf16[640,384]{1,0:T(8,128)(2,1)S(1)} %bitcast.22, f32[640,1536]{1,0:T(8,128)} %copy-done.1, bf16[640,384]{1,0:T(8,128)(2,1)S(1)} %bitcast.24, bf16[1536,384]{1,0:T(8,128)(2,1)S(1)} %copy-done.7), kind=kOutput, calls=%fused_computation.22 | convolution fusion | flops 1519779840 | bytes 8454144 | tf_op jit(solution)/shard_map/dot_general | solution.py:138
  145.0 0.0 all-reduce.5.cloned.1.call-update
  145.0 272.6 %all-reduce.5.cloned.1.call-done = (f32[1536,384]{1,0:T(8,128)}, f32[1536,384]{1,0:T(8,128)}) async-done(((f32[1536,384]{1,0:T(8,128)}, f32[1536,384]{1,0:T(8,128)}), (f32[1536,384]{1,0:T(8,128)}, f32[1536,384]{1,0:T(8,128)})) %all-reduce.5.cloned.1.call-update) | async-done | bytes 4718608
  417.6 1.4 constant_dynamic-slice_fusion
  (6 shorter events, 0.0 us)
Async XLA Ops:
  7.2 125.7 %copy-start = (bf16[1536,384]{1,0:T(8,128)(2,1)S(1)}, bf16[1536,384]{1,0:T(8,128)(2,1)}, u32[]{:S(2)}) copy-start(bf16[1536,384]{1,0:T(8,128)(2,1)} %param.22) | copy-start | bytes 3538948
  8.6 65.2 %all-to-all-start.1 = ((bf16[16,1,1]{2,1,0:T(2,128)(2,1)}), bf16[16,1,1]{2,1,0:T(2,128)(2,1)S(1)}, u32[]{:S(2)}, u32[]{:S(2)}) async-start(bf16[16,1,1]{2,1,0:T(2,128)(2,1)} %copy.23), calls=%async_computation.1 | async-start | bytes 16384 | tf_op jit(solution)/shard_map/all_to_all | solution.py:109
  16.8 32.6 %copy-start.3 = (f32[384]{0:T(512)S(1)}, f32[384]{0:T(512)}, u32[]{:S(2)}) copy-start(f32[384]{0:T(512)} %param.19) | copy-start | bytes 4612
  49.4 3.4 copy-start.5
  49.4 3.4 copy-start.6
  55.7 6.6 %copy-start.4 = (f32[384]{0:T(512)S(1)}, f32[384]{0:T(512)}, u32[]{:S(2)}) copy-start(f32[384]{0:T(512)} %param.25) | copy-start | bytes 4612
  102.2 30.7 %copy-start.2 = (f32[1536]{0:T(1024)S(1)}, f32[1536]{0:T(1024)}, u32[]{:S(2)}) copy-start(f32[1536]{0:T(1024)} %param.23) | copy-start | bytes 18436
  102.2 28.0 %all-to-all-start = ((bf16[16,128,384]{2,1,0:T(8,128)(2,1)}), bf16[16,128,384]{2,1,0:T(8,128)(2,1)S(1)}, u32[]{:S(2)}, u32[]{:S(2)}) async-start(bf16[16,128,384]{2,1,0:T(8,128)(2,1)} %get-tuple-element.14), calls=%async_computation | async-start | bytes 3145728 | tf_op jit(solution)/shard_map/all_to_all | solution.py:108
  108.3 309.2 %all-reduce.5.cloned.1.call-start = ((), (), s32[]{:S(2)}) async-start(), calls=%async_computation.3 | async-start | bytes 9437184
  134.1 1.9 copy-start.1
  136.0 2.6 copy-start.7
Sparse Core Ops, SparseCore 0:
  145.1 272.4 all-reduce.4
where the time goes:
time: 426 us
  waiting for transfers between devices  291 us (68%)
  matrix products  42.7 us (10%)
  blocking collectives  28.3 us (7%)
  other arithmetic  18.3 us (4%)
  local copies, waits for them, and re-layouts  17.2 us (4%)
  between operations  14.8 us (3%)
  starting transfers between devices  13.8 us (3%)
    unnamed x2, waiting for transfers between devices  273 us
    conv_general_dilated x1, matrix products, prepare(): lax.conv_general_dilated(tile_images, kernel, (1, 1), ((margin, margin),...  32.6 us
    all_to_all x1, blocking collectives, per_device(): lax.all_to_all(send_in, 'slide', split_axis=0, concat_axis=0, tiled=True)  28.3 us
    all_to_all x1, waiting for transfers between devices, per_device(): lax.all_to_all(send_err, 'slide', split_axis=0, concat_axis=0, tiled=True)  18 us
  transfers between devices with their start and end apart: 3, of which 2 were waited for; matrix products, arithmetic and copies ran while one was open for 14% of the time, Pallas kernels for 0%

commit v1 on v0

v1 whole, which is shorter than its diff:
```python
import functools

import jax
import jax.numpy as jnp
from jax import lax
from jax.experimental import pallas as pl
from jax.experimental.pallas import tpu as pltpu
from jax.sharding import PartitionSpec as P

BANDS = 8
BAND_ROWS = 4
BAND_TOK = 128
SLOTS = 16
GROUP = 2
HID_STEP = 512

root_half = 0.7071067811865476
inv_root_tau = 0.3989422804014327

INNER = (((1,), (1,)), ((), ()))
PLAIN = (((1,), (0,)), ((), ()))


def local_kernel(
    slots_ref,
    count_ref,
    core_ref,
    images_hbm,
    cotan_hbm,
    taps_ref,
    depth_bias_ref,
    gain_ref,
    norm_bias_ref,
    scale_ref,
    expand_ref,
    expand_bias_ref,
    project_ref,
    keep_ref,
    send_ref,
    padded,
    cotans,
    normed,
    scaled,
    conv_out,
    grad_in,
    grad_out,
    order_ref,
    sems,
):
    tiles, side, _, channels = images_hbm.shape
    margin = 3
    hidden = expand_ref.shape[0]
    held = count_ref[0]

    def image_copy(tile):
        return pltpu.make_async_copy(
            images_hbm.at[tile], padded.at[tile, pl.ds(margin, side)], sems.at[0, tile]
        )

    def cotan_copy(tile):
        return pltpu.make_async_copy(cotan_hbm.at[tile], cotans.at[tile], sems.at[1, tile])

    for tile in range(tiles):
        image_copy(tile).start()
    for tile in range(tiles):
        cotan_copy(tile).start()

    listed = jnp.int32(0)
    for slot in range(SLOTS):
        block = slots_ref[slot]
        order_ref[listed] = jnp.maximum(block, 0)
        listed = listed + jnp.where(block >= 0, 1, 0)

    for tile in range(tiles):
        padded[tile, :margin] = jnp.zeros((margin, side, channels), padded.dtype)
        padded[tile, margin + side :] = jnp.zeros((margin, side, channels), padded.dtype)
    grad_in[...] = jnp.zeros(grad_in.shape, jnp.float32)
    grad_out[...] = jnp.zeros(grad_out.shape, jnp.float32)

    for tile in range(tiles):
        image_copy(tile).wait()
    for tile in range(tiles):
        cotan_copy(tile).wait()

    scale = scale_ref[...] / held.astype(jnp.float32)
    column = lax.broadcasted_iota(jnp.int32, (side, 128), 0)
    inside = {
        dx: (column + dx >= 0) & (column + dx < side) for dx in range(-margin, margin + 1)
    }

    @pl.loop(0, listed)
    def _(index):
        block = order_ref[index]
        tile = block // BANDS
        first = (block % BANDS) * BAND_ROWS
        for lanes in range(0, channels, 128):
            part = pl.ds(lanes, 128)
            for row in range(BAND_ROWS):
                sums = [None] * 7
                for dy in range(7):
                    x = padded[tile, first + (row + dy), :, part].astype(jnp.float32)
                    for dx in range(7):
                        term = x * taps_ref[dy * 7 + dx : dy * 7 + dx + 1, part]
                        sums[dx] = term if sums[dx] is None else sums[dx] + term
                total = sums[margin] + depth_bias_ref[:, part]
                for dx in range(-margin, margin + 1):
                    if dx != 0:
                        moved = pltpu.roll(sums[dx + margin], (-dx) % side, 0)
                        total = total + jnp.where(inside[dx], moved, 0.0)
                conv_out[row * side : (row + 1) * side, part] = total
        mixed = conv_out[...]
        centre = jnp.mean(mixed, axis=-1, keepdims=True)
        away = mixed - centre
        spread = jnp.mean(away * away, axis=-1, keepdims=True)
        rows = pl.ds(pl.multiple_of(index * BAND_TOK, BAND_TOK), BAND_TOK)
        normed[rows, :] = (
            away * lax.rsqrt(spread + 1e-06) * gain_ref[...] + norm_bias_ref[...]
        ).astype(normed.dtype)
        err = cotans[tile, pl.ds(first, BAND_ROWS)].reshape(BAND_TOK, channels)
        scaled[rows, :] = (err.astype(jnp.float32) * scale).astype(scaled.dtype)

    @pl.when(listed % GROUP != 0)
    def _():
        rows = pl.ds(pl.multiple_of(listed * BAND_TOK, BAND_TOK), BAND_TOK)
        normed[rows, :] = jnp.zeros((BAND_TOK, channels), normed.dtype)
        scaled[rows, :] = jnp.zeros((BAND_TOK, channels), scaled.dtype)

    span = GROUP * BAND_TOK

    @pl.loop(0, (listed + GROUP - 1) // GROUP)
    def _(group):
        rows = pl.ds(pl.multiple_of(group * span, span), span)
        flat_in = normed[rows, :]
        flat_err = scaled[rows, :]
        for start in range(0, hidden, HID_STEP):
            units = pl.ds(start, HID_STEP)
            pre_act = lax.dot_general(
                expand_ref[units, :], flat_in, INNER, preferred_element_type=jnp.float32
            )
            back_grad = lax.dot_general(
                project_ref[units, :], flat_err, INNER, preferred_element_type=jnp.float32
            )
            pre_act = pre_act + expand_bias_ref[units, :]
            share = 0.5 * (1.0 + lax.erf(pre_act * root_half))
            activated = (pre_act * share).astype(jnp.bfloat16)
            bell = jnp.exp(-0.5 * pre_act * pre_act) * inv_root_tau
            slope_term = (back_grad * (share + pre_act * bell)).astype(jnp.bfloat16)
            grad_in[units, :] += lax.dot_general(
                slope_term, flat_in, PLAIN, preferred_element_type=jnp.float32
            )
            grad_out[units, :] += lax.dot_general(
                activated, flat_err, PLAIN, preferred_element_type=jnp.float32
            )

    core = core_ref[0]
    rows = hidden // SLOTS
    for pair in range(SLOTS // 2):
        mine = pl.ds(pl.multiple_of((2 * pair + core) * rows, rows), rows)
        other = pl.ds(pl.multiple_of((2 * pair + 1 - core) * rows, rows), rows)
        for which, grad in enumerate((grad_in, grad_out)):
            keep_ref[which, pair] = grad[mine, :]
            send_ref[which, pair] = grad[other, :].astype(send_ref.dtype)


def local_grads(
    slots,
    count,
    core,
    tile_images,
    cotangent,
    depth_kernel,
    depth_bias,
    norm_gain,
    norm_bias,
    expand_weight,
    expand_bias,
    project_weight,
    layer_scale,
):
    tiles, side, _, channels = tile_images.shape
    hidden = expand_weight.shape[0]
    rows = hidden // SLOTS
    row = lambda v: v.reshape(1, -1)
    smem = pl.BlockSpec(memory_space=pltpu.SMEM)
    vmem = pl.BlockSpec(memory_space=pltpu.VMEM)
    hbm = pl.BlockSpec(memory_space=pl.ANY)
    return pl.pallas_call(
        local_kernel,
        out_shape=(
            jax.ShapeDtypeStruct((2, SLOTS // 2, rows, channels), jnp.float32),
            jax.ShapeDtypeStruct((2, SLOTS // 2, rows, channels), jnp.bfloat16),
        ),
        in_specs=[smem] * 3 + [hbm] * 2 + [vmem] * 8,
        out_specs=[vmem] * 2,
        scratch_shapes=[
            pltpu.VMEM((tiles, side + 6, side, channels), jnp.bfloat16),
            pltpu.VMEM((tiles, side, side, channels), jnp.bfloat16),
            pltpu.VMEM((SLOTS * BAND_TOK, channels), jnp.bfloat16),
            pltpu.VMEM((SLOTS * BAND_TOK, channels), jnp.bfloat16),
            pltpu.VMEM((BAND_TOK, channels), jnp.float32),
            pltpu.VMEM((hidden, channels), jnp.float32),
            pltpu.VMEM((hidden, channels), jnp.float32),
            pltpu.SMEM((SLOTS + 1,), jnp.int32),
            pltpu.SemaphoreType.DMA((2, tiles)),
        ],
        compiler_params=pltpu.CompilerParams(vmem_limit_bytes=56 * 2**20),
        name="local_grads",
    )(
        slots,
        count,
        core,
        tile_images,
        cotangent,
        depth_kernel.reshape(-1, channels).astype(jnp.float32),
        row(depth_bias),
        row(norm_gain),
        row(norm_bias),
        row(layer_scale),
        expand_weight,
        expand_bias.reshape(-1, 1),
        project_weight,
    )


def spread_sum(total, axis_index, axis_size, link, target):
    own = lax.dynamic_index_in_dim(total, axis_index, 0, keepdims=False)
    got = []
    for step in range(1, axis_size):
        away = lax.dynamic_index_in_dim(
            total, lax.rem(axis_index + step, axis_size), 0, keepdims=False
        )
        got.append(target(away.astype(link), step))
    for piece in got:
        own = own + piece.astype(jnp.float32)
    return own


def reduce_all(keep, send):
    channels = keep.shape[-1]
    slide, rep = lax.axis_index("slide"), lax.axis_index("rep")
    from_core = lax.ppermute(send, "slide", [(i, i ^ 1) for i in range(16)])
    total = keep + from_core.astype(jnp.float32)
    total = total.reshape(2, 4, 2, -1, channels).transpose(1, 0, 2, 3, 4)
    total = spread_sum(
        total,
        slide // 4,
        4,
        jnp.bfloat16,
        lambda a, k: lax.ppermute(a, "slide", [(i, (i + 4 * k) % 16) for i in range(16)]),
    )
    total = total.reshape(2, 2, 8, 2, -1, channels).transpose(1, 3, 0, 2, 4, 5)
    total = total.reshape((4,) + total.shape[2:])
    place = (slide // 2) % 2 * 2 + rep % 2

    def along_y(a, k):
        pairs = []
        for s in range(16):
            for r in range(16):
                y = (s // 2) % 2 * 2 + r % 2
                to = (y + k) % 4
                pairs.append((s * 16 + r, ((s & ~2) | (to // 2 * 2)) * 16 + ((r & ~1) | to % 2)))
        return lax.ppermute(a, ("slide", "rep"), pairs)

    total = spread_sum(total, place, 4, jnp.bfloat16, along_y)
    total = total.transpose(1, 0, 2, 3)
    total = spread_sum(
        total,
        rep // 2,
        8,
        jnp.float32,
        lambda a, k: lax.ppermute(a, "rep", [(i, (i + 2 * k) % 16) for i in range(16)]),
    )
    return total[0], total[1]


def per_device(
    tile_images,
    cotangent,
    depth_kernel,
    depth_bias,
    norm_gain,
    norm_bias,
    expand_weight,
    expand_bias,
    project_weight,
    layer_scale,
    tile_counts,
    send_list,
):
    core = lax.rem(lax.axis_index("slide"), 2).astype(jnp.int32)
    keep, send = local_grads(
        send_list.reshape(-1),
        tile_counts.reshape(-1),
        core.reshape(1),
        tile_images,
        cotangent,
        depth_kernel,
        depth_bias,
        norm_gain,
        norm_bias,
        expand_weight,
        expand_bias,
        project_weight,
        layer_scale,
    )
    return reduce_all(keep, send)


def solution(mesh):
    in_specs = (
        P(("slide", "rep"), None, None, None),
        P(("slide", "rep"), None, None, None),
        P(),
        P(),
        P(),
        P(),
        P(),
        P(),
        P(),
        P(),
        P("slide", "rep"),
        P("slide", "rep", None),
    )
    out_specs = (P(("slide", "rep"), None), P(("slide", "rep"), None))
    return jax.shard_map(
        per_device, mesh=mesh, in_specs=in_specs, out_specs=out_specs, check_vma=False
    )
```

time: 426 us -> 102 us (0.24)
  waiting for transfers between devices: 291 us -> 25.4 us
  matrix products: 42.7 us -> 0 us
  starting transfers between devices: 13.8 us -> 48.4 us
  blocking collectives: 28.3 us -> 0 us
  other arithmetic: 18.3 us -> 3.87 us
  between operations: 14.8 us -> 1.51 us
  Pallas kernels: 0 us -> 11.1 us
  local copies, waits for them, and re-layouts: 17.2 us -> 10.1 us
    unnamed x2 -> x0, waiting for transfers between devices: 273 us -> none
    ppermute x0 -> x14, starting transfers between devices: none -> 48.4 us  [the longest x7 34.5 us: reduce_all(): lax.ppermute(a, 'rep', [(i, (i + 2 * k) % 16) for i in range(16)])]
    conv_general_dilated x1 -> x0, matrix products: 32.6 us -> none  [prepare(): lax.conv_general_dilated(tile_images, kernel, (1, 1), ((margin, margin),...]
    all_to_all x1 -> x0, blocking collectives: 28.3 us -> none  [per_device(): lax.all_to_all(send_in, 'slide', split_axis=0, concat_axis=0, tiled=True)]
    ppermute x0 -> x14, waiting for transfers between devices: none -> 25.4 us  [the longest x3 11.7 us: reduce_all(): lax.ppermute(a, 'slide', [(i, (i + 4 * k) % 16) for i in range(16)])]
    all_to_all x2 -> x0, waiting for transfers between devices: 18 us -> none  [the longest x1 18 us: per_device(): lax.all_to_all(send_err, 'slide', split_axis=0, concat_axis=0, tiled=True)]
    all_to_all x2 -> x0, starting transfers between devices: 13.6 us -> none  [the longest x1 7.48 us: per_device(): lax.all_to_all(flags, 'slide', split_axis=0, concat_axis=0, tiled=True)]
    gather x4 -> x0, local copies, waits for them, and re-layouts: 11.1 us -> none  [the longest x1 3.82 us: per_device(): jnp.take(scaled, chosen, axis=0)]
  transfers between devices with their start and end apart: 3 -> 14, of which waited for: 2 -> 9; matrix products, arithmetic and copies ran while one was open for 14% -> 1% of each run, Pallas kernels for 0% -> 0%
where the time goes in v1:
time: 102 us; the launch traced here: 100 us
  starting transfers between devices  48.4 us (47%)
  waiting for transfers between devices  25.4 us (25%)
  Pallas kernels  11.1 us (11%)
  local copies, waits for them, and re-layouts  10.1 us (10%)
  other arithmetic  3.87 us (4%)
  between operations  1.51 us (1%)
    ppermute x7, starting transfers between devices, reduce_all(): lax.ppermute(a, 'rep', [(i, (i + 2 * k) % 16) for i in range(16)])  34.5 us
    ppermute x3, waiting for transfers between devices, reduce_all(): lax.ppermute(a, 'slide', [(i, (i + 4 * k) % 16) for i in range(16)])  11.7 us
    pallas_call x1, Pallas kernels, local_grads(): pl.pallas_call(local_kernel, out_shape=(jax.ShapeDtypeStruct((2, SLOTS //...  11.1 us
    ppermute x3, starting transfers between devices, reduce_all(): lax.ppermute(a, 'slide', [(i, (i + 4 * k) % 16) for i in range(16)])  9.24 us
    ppermute x3, waiting for transfers between devices, along_y(): return lax.ppermute(a, ('slide', 'rep'), pairs)  5.4 us
    ppermute x7, waiting for transfers between devices, reduce_all(): lax.ppermute(a, 'rep', [(i, (i + 2 * k) % 16) for i in range(16)])  5.29 us
    reshape x4, local copies, waits for them, and re-layouts, local_grads(): row = lambda v: v.reshape(1, -1)  5.01 us
    ppermute x3, starting transfers between devices, along_y(): return lax.ppermute(a, ('slide', 'rep'), pairs)  4.56 us
  transfers between devices with their start and end apart: 14, of which 9 were waited for; matrix products, arithmetic and copies ran while one was open for 1% of the time, Pallas kernels for 0%

profile of v1, /device:TPU:2, one launch (start us, length us, event | category | flops | bytes accessed | tf_op | source)
XLA Modules:
  0.0 100.3 jit_solution(9739384930328682460)
XLA Ops:
  1.3 1.4 %reshape.81.taps_ref = f32[49,384]{1,0:T(8,128)} reshape(bf16[7,7,384]{2,1,0:T(8,128)(2,1)} %param.14) | data formatting | bytes 112896 | tf_op jit(solution)/shard_map/convert_element_type | solution.py:214
  2.7 1.2 %reshape.73.depth_bias_ref = f32[1,384]{1,0:T(1,128)} reshape(f32[384]{0:T(512)} %param.15) | data formatting | bytes 3072 | tf_op jit(solution)/shard_map/reshape | solution.py:183
  4.0 1.2 %reshape.74.gain_ref = f32[1,384]{1,0:T(1,128)} reshape(f32[384]{0:T(512)} %param.16) | data formatting | bytes 3072 | tf_op jit(solution)/shard_map/reshape | solution.py:183
  5.2 1.3 %reshape.75.norm_bias_ref = f32[1,384]{1,0:T(1,128)} reshape(f32[384]{0:T(512)} %param.17) | data formatting | bytes 3072 | tf_op jit(solution)/shard_map/reshape | solution.py:183
  6.5 1.3 %reshape.76.scale_ref = f32[1,384]{1,0:T(1,128)} reshape(f32[384]{0:T(512)} %param.21) | data formatting | bytes 3072 | tf_op jit(solution)/shard_map/reshape | solution.py:183
  7.7 1.8 %reshape.82.expand_bias_ref = f32[1536,1]{1,0:T(8,128)} reshape(f32[1536]{0:T(1024)} %param.19) | data formatting | bytes 12288 | tf_op jit(solution)/shard_map/reshape | solution.py:220
  9.6 11.1 %local_grads.1 = (f32[2,8,96,384]{3,2,1,0:T(8,128)}, bf16[2,8,96,384]{3,2,1,0:T(8,128)(2,1)}) custom-call(s32[16]{0:T(128)} %bitcast.90, s32[1]{0:T(128)} %bitcast.74.count_ref, s32[1]{0:T(128)} %bitcast.2.core_ref, bf16[4,32,32,384]{3,2,1,0:T(8,128)(2,1)} %images_hbm.1, bf16[4,32,32,384]{3,2,1,0:T(8,128)(2,1)} %cotan_hbm.1, f32[49,384]{1,0:T(8,128)} %reshape.81.taps_ref, ...), custom_call_target="tpu_custom_call" | custom-call | tf_op jit(solution)/shard_map/local_grads/pallas_call | solution.py:187
  20.7 0.1 collective-permute-start
  20.8 3.0 %collective-permute-done = bf16[2,8,96,384]{3,2,1,0:T(8,128)(2,1)S(1)} collective-permute-done((bf16[2,8,96,384]{3,2,1,0:T(8,128)(2,1)}, bf16[2,8,96,384]{3,2,1,0:T(8,128)(2,1)S(1)}, u32[]{:S(2)}, u32[]{:S(2)}) %collective-permute-start) | collective-permute-done | bytes 1179680 | tf_op jit(solution)/shard_map/ppermute | solution.py:241
  23.8 1.9 %convert_add_fusion = f32[2,8,96,384]{3,2,1,0:T(8,128)S(1)} fusion(f32[2,8,96,384]{3,2,1,0:T(8,128)} %get-tuple-element.4, bf16[2,8,96,384]{3,2,1,0:T(8,128)(2,1)S(1)} %collective-permute-done), kind=kLoop, calls=%fused_computation | loop fusion | flops 1179648 | bytes 5898240 | tf_op jit(solution)/shard_map/add | solution.py:242
  25.7 0.1 dynamic-slice_convert_fusion.2
  25.9 0.2 copy.64
  26.1 5.6 %collective-permute-start.3 = (bf16[2,2,96,384]{3,1,2,0:T(2,128)(2,1)S(1)}, bf16[2,2,96,384]{3,1,2,0:T(2,128)(2,1)S(1)}, u32[]{:S(2)}, u32[]{:S(2)}) collective-permute-start(bf16[2,2,96,384]{3,1,2,0:T(2,128)(2,1)S(1)} %bitcast.80), channel_id=1, source_target_pairs={{0,192},{16,208},{32,224},{48,240},{64,0},{80,16},{96,32},{112,48}... | collective-permute-start | bytes 884744 | tf_op jit(solution)/shard_map/ppermute | solution.py:249
  31.7 0.2 copy.65
  31.9 0.9 collective-permute-start.2
  32.9 0.2 copy.66
  33.1 2.7 %collective-permute-start.1 = (bf16[2,2,96,384]{3,1,2,0:T(2,128)(2,1)S(1)}, bf16[2,2,96,384]{3,1,2,0:T(2,128)(2,1)}, u32[]{:S(2)}, u32[]{:S(2)}) collective-permute-start(bf16[2,2,96,384]{3,1,2,0:T(2,128)(2,1)S(1)} %bitcast.82), channel_id=1, source_target_pairs={{0,64},{16,80},{32,96},{48,112},{64,128},{80,144},{96,160},{112,17... | collective-permute-start | bytes 884744 | tf_op jit(solution)/shard_map/ppermute | solution.py:249
  35.8 3.2 %collective-permute-done.3 = bf16[2,2,96,384]{3,1,2,0:T(2,128)(2,1)S(1)} collective-permute-done((bf16[2,2,96,384]{3,1,2,0:T(2,128)(2,1)S(1)}, bf16[2,2,96,384]{3,1,2,0:T(2,128)(2,1)S(1)}, u32[]{:S(2)}, u32[]{:S(2)}) %collective-permute-start.3) | collective-permute-done | bytes 294944 | tf_op jit(solution)/shard_map/ppermute | solution.py:249
  39.1 7.2 %collective-permute-done.2 = bf16[2,2,96,384]{3,1,2,0:T(2,128)(2,1)} collective-permute-done((bf16[2,2,96,384]{3,1,2,0:T(2,128)(2,1)S(1)}, bf16[2,2,96,384]{3,1,2,0:T(2,128)(2,1)}, u32[]{:S(2)}, u32[]{:S(2)}) %collective-permute-start.2) | collective-permute-done | bytes 294944 | tf_op jit(solution)/shard_map/ppermute | solution.py:249
  46.3 1.3 %collective-permute-done.1 = bf16[2,2,96,384]{3,1,2,0:T(2,128)(2,1)} collective-permute-done((bf16[2,2,96,384]{3,1,2,0:T(2,128)(2,1)S(1)}, bf16[2,2,96,384]{3,1,2,0:T(2,128)(2,1)}, u32[]{:S(2)}, u32[]{:S(2)}) %collective-permute-start.1) | collective-permute-done | bytes 294944 | tf_op jit(solution)/shard_map/ppermute | solution.py:249
  47.5 1.9 %fusion.1 = f32[2,2,96,384]{3,1,2,0:T(2,128)S(1)} fusion(f32[2,1,2,96,384]{4,3,2,1,0:T(8,128)S(1)} %constant_dynamic-slice_fusion.8, bf16[2,2,96,384]{3,1,2,0:T(2,128)(2,1)S(1)} %collective-permute-done.3, bf16[2,2,96,384]{3,1,2,0:T(2,128)(2,1)} %collective-permute-done.2, bf16[2,2,96,384]{3,1,2,0:T(2,128)(2,1)} %collective-permute-done.1), kind=kLoop, calls=%fused_computation.3 | loop fusion | flops 884736 | bytes 2064384 | tf_op jit(solution)/shard_map/add | solution.py:234
  49.4 0.1 copy.33
  49.6 3.6 %collective-permute-start.6 = (bf16[2,8,6,384]{3,1,2,0:T(8,128)(2,1)S(1)}, bf16[2,8,6,384]{3,1,2,0:T(8,128)(2,1)S(1)}, u32[]{:S(2)}, u32[]{:S(2)}) collective-permute-start(bf16[2,8,6,384]{3,1,2,0:T(8,128)(2,1)S(1)} %get-tuple-element.10), channel_id=1, source_target_pairs={{0,33},{1,0},{2,35},{3,2},{4,37},{5,4},{6,39},{7,6},{8,41},{9,8},{... | collective-permute-start | bytes 221192 | tf_op jit(solution)/shard_map/ppermute | solution.py:262
  53.2 0.0 collective-permute-start.5
  53.2 1.0 collective-permute-start.4
  54.1 1.7 %collective-permute-done.6 = bf16[2,8,6,384]{3,1,2,0:T(8,128)(2,1)S(1)} collective-permute-done((bf16[2,8,6,384]{3,1,2,0:T(8,128)(2,1)S(1)}, bf16[2,8,6,384]{3,1,2,0:T(8,128)(2,1)S(1)}, u32[]{:S(2)}, u32[]{:S(2)}) %collective-permute-start.6) | collective-permute-done | bytes 73760 | tf_op jit(solution)/shard_map/ppermute | solution.py:262
  55.9 3.3 %collective-permute-done.5 = bf16[2,8,6,384]{3,1,2,0:T(8,128)(2,1)S(1)} collective-permute-done((bf16[2,8,6,384]{3,1,2,0:T(8,128)(2,1)S(1)}, bf16[2,8,6,384]{3,1,2,0:T(8,128)(2,1)S(1)}, u32[]{:S(2)}, u32[]{:S(2)}) %collective-permute-start.5) | collective-permute-done | bytes 73760 | tf_op jit(solution)/shard_map/ppermute | solution.py:262
  59.1 0.4 collective-permute-done.4
  59.6 0.1 constant_dynamic-slice_fusion.7
  59.7 5.4 %collective-permute-start.13 = (f32[2,6,384]{2,0,1:T(2,128)S(1)}, f32[2,6,384]{2,0,1:T(2,128)S(1)}, u32[]{:S(2)}, u32[]{:S(2)}) collective-permute-start(f32[2,6,384]{2,0,1:T(2,128)S(1)} %bitcast.86), channel_id=1, source_target_pairs={{0,14},{1,15},{2,0},{3,1},{4,2},{5,3},{6,4},{7,5},{8,6},{9,7},{10,... | collective-permute-start | bytes 55304 | tf_op jit(solution)/shard_map/ppermute | solution.py:271
  65.1 2.5 %collective-permute-start.12 = (f32[2,6,384]{2,0,1:T(2,128)S(1)}, f32[2,6,384]{2,0,1:T(2,128)S(1)}, u32[]{:S(2)}, u32[]{:S(2)}) collective-permute-start(f32[2,6,384]{2,0,1:T(2,128)S(1)} %bitcast.84), channel_id=1, source_target_pairs={{0,12},{1,13},{2,14},{3,15},{4,0},{5,1},{6,2},{7,3},{8,4},{9,5},{1... | collective-permute-start | bytes 55304 | tf_op jit(solution)/shard_map/ppermute | solution.py:271
  67.7 0.1 collective-permute-start.11
  67.8 22.0 %collective-permute-start.10 = (f32[2,6,384]{2,0,1:T(2,128)S(1)}, f32[2,6,384]{2,0,1:T(2,128)S(1)}, u32[]{:S(2)}, u32[]{:S(2)}) collective-permute-start(f32[2,6,384]{2,0,1:T(2,128)S(1)} %bitcast.85), channel_id=1, source_target_pairs={{0,8},{1,9},{2,10},{3,11},{4,12},{5,13},{6,14},{7,15},{8,0},{9,1},... | collective-permute-start | bytes 55304 | tf_op jit(solution)/shard_map/ppermute | solution.py:271
  89.8 3.9 %collective-permute-start.9 = (f32[2,6,384]{2,0,1:T(2,128)S(1)}, f32[2,6,384]{2,0,1:T(2,128)S(1)}, u32[]{:S(2)}, u32[]{:S(2)}) collective-permute-start(f32[2,6,384]{2,0,1:T(2,128)S(1)} %bitcast.87), channel_id=1, source_target_pairs={{0,6},{1,7},{2,8},{3,9},{4,10},{5,11},{6,12},{7,13},{8,14},{9,15},... | collective-permute-start | bytes 55304 | tf_op jit(solution)/shard_map/ppermute | solution.py:271
  93.7 0.0 collective-permute-done.13
  93.7 0.1 collective-permute-start.8
  93.8 0.0 collective-permute-done.12
  93.8 0.6 collective-permute-start.7
  94.3 0.0 collective-permute-done.11
  94.4 0.0 collective-permute-done.10
  94.4 2.3 %collective-permute-done.9 = f32[2,6,384]{2,0,1:T(2,128)S(1)} collective-permute-done((f32[2,6,384]{2,0,1:T(2,128)S(1)}, f32[2,6,384]{2,0,1:T(2,128)S(1)}, u32[]{:S(2)}, u32[]{:S(2)}) %collective-permute-start.9) | collective-permute-done | bytes 18464 | tf_op jit(solution)/shard_map/ppermute | solution.py:271
  96.6 3.0 %collective-permute-done.8 = f32[2,6,384]{2,0,1:T(2,128)S(1)} collective-permute-done((f32[2,6,384]{2,0,1:T(2,128)S(1)}, f32[2,6,384]{2,0,1:T(2,128)S(1)}, u32[]{:S(2)}, u32[]{:S(2)}) %collective-permute-start.8) | collective-permute-done | bytes 18464 | tf_op jit(solution)/shard_map/ppermute | solution.py:271
  99.6 0.0 collective-permute-done.7
  99.7 0.6 copy_bitcast_fusion.10
  (12 shorter events, 0.2 us)
Async XLA Ops:
  20.7 3.1 %collective-permute-start = (bf16[2,8,96,384]{3,2,1,0:T(8,128)(2,1)}, bf16[2,8,96,384]{3,2,1,0:T(8,128)(2,1)S(1)}, u32[]{:S(2)}, u32[]{:S(2)}) collective-permute-start(bf16[2,8,96,384]{3,2,1,0:T(8,128)(2,1)} %get-tuple-element.5), channel_id=1, source_target_pairs={{0,16},{16,0},{32,48},{48,32},{64,80},{80,64},{96,112},{112,96},{1... | collective-permute-start | bytes 3538952 | tf_op jit(solution)/shard_map/ppermute | solution.py:241
  26.1 13.0 %collective-permute-start.3 = (bf16[2,2,96,384]{3,1,2,0:T(2,128)(2,1)S(1)}, bf16[2,2,96,384]{3,1,2,0:T(2,128)(2,1)S(1)}, u32[]{:S(2)}, u32[]{:S(2)}) collective-permute-start(bf16[2,2,96,384]{3,1,2,0:T(2,128)(2,1)S(1)} %bitcast.80), channel_id=1, source_target_pairs={{0,192},{16,208},{32,224},{48,240},{64,0},{80,16},{96,32},{112,48}... | collective-permute-start | bytes 884744 | tf_op jit(solution)/shard_map/ppermute | solution.py:249
  31.9 14.3 %collective-permute-start.2 = (bf16[2,2,96,384]{3,1,2,0:T(2,128)(2,1)S(1)}, bf16[2,2,96,384]{3,1,2,0:T(2,128)(2,1)}, u32[]{:S(2)}, u32[]{:S(2)}) collective-permute-start(bf16[2,2,96,384]{3,1,2,0:T(2,128)(2,1)S(1)} %bitcast.81), channel_id=1, source_target_pairs={{0,128},{16,144},{32,160},{48,176},{64,192},{80,208},{96,224},{112... | collective-permute-start | bytes 884744 | tf_op jit(solution)/shard_map/ppermute | solution.py:249
  33.1 14.4 %collective-permute-start.1 = (bf16[2,2,96,384]{3,1,2,0:T(2,128)(2,1)S(1)}, bf16[2,2,96,384]{3,1,2,0:T(2,128)(2,1)}, u32[]{:S(2)}, u32[]{:S(2)}) collective-permute-start(bf16[2,2,96,384]{3,1,2,0:T(2,128)(2,1)S(1)} %bitcast.82), channel_id=1, source_target_pairs={{0,64},{16,80},{32,96},{48,112},{64,128},{80,144},{96,160},{112,17... | collective-permute-start | bytes 884744 | tf_op jit(solution)/shard_map/ppermute | solution.py:249
  49.6 6.3 %collective-permute-start.6 = (bf16[2,8,6,384]{3,1,2,0:T(8,128)(2,1)S(1)}, bf16[2,8,6,384]{3,1,2,0:T(8,128)(2,1)S(1)}, u32[]{:S(2)}, u32[]{:S(2)}) collective-permute-start(bf16[2,8,6,384]{3,1,2,0:T(8,128)(2,1)S(1)} %get-tuple-element.10), channel_id=1, source_target_pairs={{0,33},{1,0},{2,35},{3,2},{4,37},{5,4},{6,39},{7,6},{8,41},{9,8},{... | collective-permute-start | bytes 221192 | tf_op jit(solution)/shard_map/ppermute | solution.py:262
  53.2 6.0 %collective-permute-start.5 = (bf16[2,8,6,384]{3,1,2,0:T(8,128)(2,1)S(1)}, bf16[2,8,6,384]{3,1,2,0:T(8,128)(2,1)S(1)}, u32[]{:S(2)}, u32[]{:S(2)}) collective-permute-start(bf16[2,8,6,384]{3,1,2,0:T(8,128)(2,1)S(1)} %get-tuple-element.11), channel_id=1, source_target_pairs={{0,32},{1,33},{2,34},{3,35},{4,36},{5,37},{6,38},{7,39},{8,40},{9,... | collective-permute-start | bytes 221192 | tf_op jit(solution)/shard_map/ppermute | solution.py:262
  53.2 6.4 %collective-permute-start.4 = (bf16[2,8,6,384]{3,1,2,0:T(8,128)(2,1)S(1)}, bf16[2,8,6,384]{3,1,2,0:T(8,128)(2,1)S(1)}, u32[]{:S(2)}, u32[]{:S(2)}) collective-permute-start(bf16[2,8,6,384]{3,1,2,0:T(8,128)(2,1)S(1)} %get-tuple-element.9), channel_id=1, source_target_pairs={{0,1},{1,32},{2,3},{3,34},{4,5},{5,36},{6,7},{7,38},{8,9},{9,40},{... | collective-permute-start | bytes 221192 | tf_op jit(solution)/shard_map/ppermute | solution.py:262
  59.7 34.0 %collective-permute-start.13 = (f32[2,6,384]{2,0,1:T(2,128)S(1)}, f32[2,6,384]{2,0,1:T(2,128)S(1)}, u32[]{:S(2)}, u32[]{:S(2)}) collective-permute-start(f32[2,6,384]{2,0,1:T(2,128)S(1)} %bitcast.86), channel_id=1, source_target_pairs={{0,14},{1,15},{2,0},{3,1},{4,2},{5,3},{6,4},{7,5},{8,6},{9,7},{10,... | collective-permute-start | bytes 55304 | tf_op jit(solution)/shard_map/ppermute | solution.py:271
  65.1 28.6 %collective-permute-start.12 = (f32[2,6,384]{2,0,1:T(2,128)S(1)}, f32[2,6,384]{2,0,1:T(2,128)S(1)}, u32[]{:S(2)}, u32[]{:S(2)}) collective-permute-start(f32[2,6,384]{2,0,1:T(2,128)S(1)} %bitcast.84), channel_id=1, source_target_pairs={{0,12},{1,13},{2,14},{3,15},{4,0},{5,1},{6,2},{7,3},{8,4},{9,5},{1... | collective-permute-start | bytes 55304 | tf_op jit(solution)/shard_map/ppermute | solution.py:271
  67.7 26.7 %collective-permute-start.11 = (f32[2,6,384]{2,0,1:T(2,128)S(1)}, f32[2,6,384]{2,0,1:T(2,128)S(1)}, u32[]{:S(2)}, u32[]{:S(2)}) collective-permute-start(f32[2,6,384]{2,0,1:T(2,128)S(1)} %bitcast.83), channel_id=1, source_target_pairs={{0,10},{1,11},{2,12},{3,13},{4,14},{5,15},{6,0},{7,1},{8,2},{9,3},... | collective-permute-start | bytes 55304 | tf_op jit(solution)/shard_map/ppermute | solution.py:271
  67.8 26.6 %collective-permute-start.10 = (f32[2,6,384]{2,0,1:T(2,128)S(1)}, f32[2,6,384]{2,0,1:T(2,128)S(1)}, u32[]{:S(2)}, u32[]{:S(2)}) collective-permute-start(f32[2,6,384]{2,0,1:T(2,128)S(1)} %bitcast.85), channel_id=1, source_target_pairs={{0,8},{1,9},{2,10},{3,11},{4,12},{5,13},{6,14},{7,15},{8,0},{9,1},... | collective-permute-start | bytes 55304 | tf_op jit(solution)/shard_map/ppermute | solution.py:271
  89.8 6.9 %collective-permute-start.9 = (f32[2,6,384]{2,0,1:T(2,128)S(1)}, f32[2,6,384]{2,0,1:T(2,128)S(1)}, u32[]{:S(2)}, u32[]{:S(2)}) collective-permute-start(f32[2,6,384]{2,0,1:T(2,128)S(1)} %bitcast.87), channel_id=1, source_target_pairs={{0,6},{1,7},{2,8},{3,9},{4,10},{5,11},{6,12},{7,13},{8,14},{9,15},... | collective-permute-start | bytes 55304 | tf_op jit(solution)/shard_map/ppermute | solution.py:271
  93.7 5.9 %collective-permute-start.8 = (f32[2,6,384]{2,0,1:T(2,128)S(1)}, f32[2,6,384]{2,0,1:T(2,128)S(1)}, u32[]{:S(2)}, u32[]{:S(2)}) collective-permute-start(f32[2,6,384]{2,0,1:T(2,128)S(1)} %bitcast.89), channel_id=1, source_target_pairs={{0,4},{1,5},{2,6},{3,7},{4,8},{5,9},{6,10},{7,11},{8,12},{9,13},{1... | collective-permute-start | bytes 55304 | tf_op jit(solution)/shard_map/ppermute | solution.py:271
  93.8 5.8 %collective-permute-start.7 = (f32[2,6,384]{2,0,1:T(2,128)S(1)}, f32[2,6,384]{2,0,1:T(2,128)S(1)}, u32[]{:S(2)}, u32[]{:S(2)}) collective-permute-start(f32[2,6,384]{2,0,1:T(2,128)S(1)} %bitcast.88), channel_id=1, source_target_pairs={{0,2},{1,3},{2,4},{3,5},{4,6},{5,7},{6,8},{7,9},{8,10},{9,11},{10,... | collective-permute-start | bytes 55304 | tf_op jit(solution)/shard_map/ppermute | solution.py:271
